TPU v7x, 32 devices: a whole 2x2x4 slice. The times are simulated.
32 devices in a mesh: region: 2 (over y), dom: 4 (over x, core), sub: 4 (over z).
Axes of the slice: x: 2, y: 2, z: 4, core: 2. Of those that a mesh axis runs over, the one named last changes fastest.
Arguments:
- features: bfloat16 [16384, 256], P(('region', 'dom', 'sub')), parts along dimension 0, may hold values from -6 to 6
- local_blocks: int32 [128, 4], P(('region', 'dom', 'sub')), parts along dimension 0, may hold values from 0 to 15
- local_matrix: bfloat16 [128, 4, 128, 128], P(('region', 'dom', 'sub')), parts along dimension 0, may hold values from -0.1875 to 0.1875
- remote_blocks: int32 [128, 4], P(('region', 'dom', 'sub')), parts along dimension 0, may hold values from 0 to 3
- remote_matrix: bfloat16 [128, 4, 128, 128], P(('region', 'dom', 'sub')), parts along dimension 0, may hold values from -0.1875 to 0.1875
- send_blocks: int32 [32, 2, 2], P(('region', 'dom', 'sub')), parts along dimension 0, may hold values from 0 to 3
- send_counts: int32 [32, 2], P(('region', 'dom', 'sub')), parts along dimension 0, may hold values from 1 to 2
- partner: int32 [4, 4], P('region'), parts along dimension 0, may hold values from 0 to 3, as said below
- self_weight: bfloat16 [2, 256, 512], replicated, may hold values from -0.375 to 0.375
- neighbor_weight: bfloat16 [2, 256, 512], replicated, may hold values from -0.375 to 0.375
- output_weight: bfloat16 [2, 512, 256], replicated, may hold values from -0.25 to 0.25
- output_cotangent: bfloat16 [16384, 256], P(('region', 'dom', 'sub')), parts along dimension 0, may hold values from -6 to 6
Outputs:
- updated: bfloat16 [16384, 256], P(('region', 'dom', 'sub')), parts along dimension 0
- feature_grad: float32 [16384, 256], P(('region', 'dom', 'sub')), parts along dimension 0
- self_grad: float32 [4, 256, 512], P('region'), parts along dimension 0
- neighbor_grad: float32 [4, 256, 512], P('region'), parts along dimension 0
- output_grad: float32 [4, 512, 256], P('region'), parts along dimension 0
There are 2 independent parts, one for each index of `region`. A program takes and returns all parts, laid end to end along the dimension named above; an argument that names none is the same for every part. Nothing has to cross between parts.
Inputs may be any that keep to these rules, and one draw needn't show every extreme that they name: Every round is a perfect matching of the 4 partitions (partner[r, partner[r, d]] = d, never d itself), and no two partitions are matched in two rounds.
All inputs are finite; a program needn't handle non-finite values.
Results may differ from a plain program's by a relative error of at most 0.009.
Values may be sent and summed in bfloat16 or wider, within the bound.
A program may use at most 64 MiB of HBM per device.

v0:
```python
import jax
import jax.numpy as jnp
from jax import lax
from jax.sharding import PartitionSpec as P


def local(
    features,
    local_blocks,
    local_matrix,
    remote_blocks,
    remote_matrix,
    send_blocks,
    send_counts,
    partner,
    self_weight,
    neighbor_weight,
    output_weight,
    output_cotangent,
):
    blocks_here = local_blocks.shape[0]
    block_size = local_matrix.shape[2]
    width = features.shape[1]
    layers = self_weight.shape[0]
    dom_count = lax.axis_size("dom")
    sub_count = lax.axis_size("sub")
    rounds = partner.shape[0]
    slot_count = send_blocks.shape[2]
    nodes_all = blocks_here * block_size * dom_count * sub_count
    scale = 1.0 / nodes_all**0.5
    my_dom = lax.axis_index("dom")
    my_partners = lax.dynamic_index_in_dim(partner, my_dom, 1, keepdims=False)
    routing = (my_partners[None, :] == jnp.arange(dom_count, dtype=jnp.int32)[:, None]).astype(
        jnp.bfloat16
    )
    live_mask = jnp.arange(slot_count, dtype=jnp.int32)[None, :] < send_counts[0][:, None]
    select = (
        (send_blocks[0][:, :, None] == jnp.arange(blocks_here, dtype=jnp.int32)[None, None, :])
        & live_mask[:, :, None]
    ).astype(jnp.bfloat16)
    slot_onehot = (
        remote_blocks[None, :, :] == jnp.arange(rounds * slot_count, dtype=jnp.int32)[:, None, None]
    ).astype(jnp.float32)
    saved = []
    state = features
    for layer_id in range(layers):
        partition = lax.all_gather(state, "sub", axis=0, tiled=True)
        part_blocks = partition.reshape(-1, block_size, width)
        own_blocks = state.reshape(blocks_here, block_size, width)
        outgoing = jnp.einsum(
            "rsb,bnd->rsnd", select, own_blocks, preferred_element_type=jnp.float32
        ).astype(jnp.bfloat16)
        sendbuf = jnp.einsum(
            "pr,rsnd->psnd", routing, outgoing, preferred_element_type=jnp.float32
        ).astype(jnp.bfloat16)
        arrived = lax.all_to_all(sendbuf, "dom", split_axis=0, concat_axis=0, tiled=True)
        boundary = jnp.einsum(
            "pr,psnd->rsnd", routing, arrived, preferred_element_type=jnp.float32
        ).astype(jnp.bfloat16)
        boundary = boundary.reshape(rounds * slot_count, block_size, width)
        near = part_blocks[local_blocks]
        far = boundary[remote_blocks]
        total = jnp.einsum("nkab,nkbd->nad", local_matrix, near, preferred_element_type=jnp.float32)
        total = total + jnp.einsum(
            "nkab,nkbd->nad", remote_matrix, far, preferred_element_type=jnp.float32
        )
        aggregate = total.reshape(-1, width).astype(jnp.bfloat16)
        preact = jnp.dot(
            state, self_weight[layer_id], preferred_element_type=jnp.float32
        ) + jnp.dot(aggregate, neighbor_weight[layer_id], preferred_element_type=jnp.float32)
        hidden = jax.nn.silu(preact).astype(jnp.bfloat16)
        result = (
            state.astype(jnp.float32)
            + jnp.dot(hidden, output_weight[layer_id], preferred_element_type=jnp.float32)
        ).astype(jnp.bfloat16)
        saved.append((state, aggregate, preact, hidden))
        state = result
    updated = state
    upstream = output_cotangent.astype(jnp.float32)
    grads_self = [None] * layers
    grads_neighbor = [None] * layers
    grads_output = [None] * layers
    for layer_id in range(layers - 1, -1, -1):
        state, aggregate, preact, hidden = saved[layer_id]
        cot = upstream.astype(jnp.bfloat16)
        local_output = jnp.dot(hidden.T, cot, preferred_element_type=jnp.float32)
        grad_hidden = jnp.dot(cot, output_weight[layer_id].T, preferred_element_type=jnp.float32)
        logistic = jax.nn.sigmoid(preact)
        grad_preact = (grad_hidden * logistic * (1.0 + preact * (1.0 - logistic))).astype(
            jnp.bfloat16
        )
        local_self = jnp.dot(state.T, grad_preact, preferred_element_type=jnp.float32)
        local_neighbor = jnp.dot(aggregate.T, grad_preact, preferred_element_type=jnp.float32)
        grads_self[layer_id] = local_self
        grads_neighbor[layer_id] = local_neighbor
        grads_output[layer_id] = local_output
        grad_aggregate = jnp.dot(
            grad_preact, neighbor_weight[layer_id].T, preferred_element_type=jnp.float32
        ).astype(jnp.bfloat16)
        grad_blocks = grad_aggregate.reshape(blocks_here, block_size, width)
        near_terms = jnp.einsum(
            "nkab,nad->nkbd", local_matrix, grad_blocks, preferred_element_type=jnp.float32
        )
        block_count = blocks_here * block_size * lax.axis_size("sub") // block_size
        targets = jnp.arange(block_count, dtype=jnp.int32)
        onehot = (local_blocks[None, :, :] == targets[:, None, None]).astype(jnp.float32)
        near_sum = lax.psum_scatter(
            jnp.einsum("mnk,nkbd->mbd", onehot, near_terms, precision=lax.Precision.HIGHEST)
            .reshape(blocks_here * block_size * lax.axis_size("sub"), width)
            .astype(jnp.bfloat16),
            "sub",
            scatter_dimension=0,
            tiled=True,
        ).astype(jnp.float32)
        far_terms = jnp.einsum(
            "nkab,nad->nkbd", remote_matrix, grad_blocks, preferred_element_type=jnp.float32
        )
        slot_grad = jnp.einsum(
            "qnk,nkbd->qbd", slot_onehot, far_terms, precision=lax.Precision.HIGHEST
        ).astype(jnp.bfloat16)
        slot_grad = slot_grad.reshape(rounds, slot_count, block_size, width)
        backbuf = jnp.einsum(
            "pr,rsnd->psnd", routing, slot_grad, preferred_element_type=jnp.float32
        ).astype(jnp.bfloat16)
        returned = lax.all_to_all(backbuf, "dom", split_axis=0, concat_axis=0, tiled=True)
        by_round = jnp.einsum(
            "pr,psnd->rsnd", routing, returned, preferred_element_type=jnp.float32
        ).astype(jnp.bfloat16)
        far_sum = jnp.einsum(
            "rsb,rsnd->bnd", select, by_round, preferred_element_type=jnp.float32
        ).reshape(-1, width)
        upstream = (
            upstream
            + jnp.dot(grad_preact, self_weight[layer_id].T, preferred_element_type=jnp.float32)
            + near_sum
            + far_sum
        )
    stacked_self = jnp.stack(grads_self)
    stacked_neighbor = jnp.stack(grads_neighbor)
    stacked_output = jnp.stack(grads_output)
    stacked_self, stacked_neighbor, stacked_output = lax.psum(
        (stacked_self, stacked_neighbor, stacked_output), ("dom", "sub")
    )
    stacked_self = stacked_self * scale
    stacked_neighbor = stacked_neighbor * scale
    stacked_output = stacked_output * scale
    return (updated, upstream, stacked_self, stacked_neighbor, stacked_output)


def solution(mesh):
    in_specs = (
        P(("region", "dom", "sub"), None),
        P(("region", "dom", "sub"), None),
        P(("region", "dom", "sub"), None, None, None),
        P(("region", "dom", "sub"), None),
        P(("region", "dom", "sub"), None, None, None),
        P(("region", "dom", "sub"), None, None),
        P(("region", "dom", "sub"), None),
        P("region", None),
        P(),
        P(),
        P(),
        P(("region", "dom", "sub"), None),
    )
    out_specs = (
        P(("region", "dom", "sub"), None),
        P(("region", "dom", "sub"), None),
        P("region", None, None),
        P("region", None, None),
        P("region", None, None),
    )
    return jax.shard_map(local, mesh=mesh, in_specs=in_specs, out_specs=out_specs, check_vma=False)
```

profile of v0, /device:TPU:1, one launch (start us, length us, event | category | flops | bytes accessed | tf_op | source)
XLA Modules:
  0.0 262.2 jit_solution(4357449218662043264)
XLA Ops:
  12.4 4.3 %all-to-all-start = ((bf16[4,2,128,256]{3,2,1,0:T(8,128)(2,1)}), bf16[4,2,128,256]{3,2,1,0:T(8,128)(2,1)S(1)}, u32[]{:S(2)}, u32[]{:S(2)}) async-start(bf16[4,2,128,256]{3,2,1,0:T(8,128)(2,1)} %copy.76), calls=%async_computation | async-start | bytes 1048576 | tf_op jit(solution)/shard_map/all_to_all | solution.py:56
  18.2 6.4 %all-to-all-done = bf16[4,2,128,256]{3,2,1,0:T(8,128)(2,1)S(1)} async-done(((bf16[4,2,128,256]{3,2,1,0:T(8,128)(2,1)}), bf16[4,2,128,256]{3,2,1,0:T(8,128)(2,1)S(1)}, u32[]{:S(2)}, u32[]{:S(2)}) %all-to-all-start) | async-done | bytes 524320 | tf_op jit(solution)/shard_map/all_to_all | solution.py:56
  26.9 12.6 %all-gather.3.cloned.1.call-done = bf16[2048,256]{1,0:T(8,128)(2,1)} async-done(((bf16[512,256]{1,0:T(8,128)(2,1)}), bf16[2048,256]{1,0:T(8,128)(2,1)}) %all-gather.3.cloned.1.call-update) | async-done | bytes 1048592 | tf_op jit(solution)/shard_map/all_gather | solution.py:47
  39.6 1.9 gather_fusion
  48.8 4.3 %all-to-all-start.1 = ((bf16[4,2,128,256]{3,2,1,0:T(8,128)(2,1)}), bf16[4,2,128,256]{3,2,1,0:T(8,128)(2,1)S(1)}, u32[]{:S(2)}, u32[]{:S(2)}) async-start(bf16[4,2,128,256]{3,2,1,0:T(8,128)(2,1)} %copy.81), calls=%async_computation.1 | async-start | bytes 1048576 | tf_op jit(solution)/shard_map/all_to_all | solution.py:56
  54.4 6.7 %all-to-all-done.1 = bf16[4,2,128,256]{3,2,1,0:T(8,128)(2,1)S(1)} async-done(((bf16[4,2,128,256]{3,2,1,0:T(8,128)(2,1)}), bf16[4,2,128,256]{3,2,1,0:T(8,128)(2,1)S(1)}, u32[]{:S(2)}, u32[]{:S(2)}) %all-to-all-start.1) | async-done | bytes 524320 | tf_op jit(solution)/shard_map/all_to_all | solution.py:56
  62.7 10.8 %all-gather.5.cloned.1.call-done = bf16[2048,256]{1,0:T(8,128)(2,1)} async-done(((bf16[512,256]{1,0:T(8,128)(2,1)}), bf16[2048,256]{1,0:T(8,128)(2,1)}) %all-gather.5.cloned.1.call-update) | async-done | bytes 1048592 | tf_op jit(solution)/shard_map/all_gather | solution.py:47
  73.5 1.8 gather_fusion.2
  79.6 1.8 convolution_bitcast_fusion.3
  81.4 2.4 copy.86
  83.8 1.7 bitcast_convert_fusion.1
  88.4 2.1 copy.90
  90.5 3.4 %fusion.14 = bf16[4,128,256]{2,0,1:T(4,128)(2,1)S(1)} fusion(f32[4,4,128,256]{3,0,1,2:T(4,128)} %copy.90, s32[4,4]{0,1:T(4,128)S(1)} %copy.88), kind=kOutput, calls=%fused_computation.50 | convolution fusion | flops 25296960 | bytes 2359360 | tf_op jit(solution)/shard_map/qnk,nkbd->qbd/dot_general | solution.py:118
  95.4 5.0 %all-to-all-start.2 = ((bf16[4,2,128,256]{3,2,1,0:T(8,128)(2,1)}), bf16[4,2,128,256]{3,2,1,0:T(8,128)(2,1)}, u32[]{:S(2)}, u32[]{:S(2)}) async-start(bf16[4,2,128,256]{3,2,1,0:T(8,128)(2,1)} %copy.92), calls=%async_computation.3 | async-start | bytes 1048576 | tf_op jit(solution)/shard_map/all_to_all | solution.py:125
  103.1 5.4 %all-to-all-done.2 = bf16[4,2,128,256]{3,2,1,0:T(8,128)(2,1)} async-done(((bf16[4,2,128,256]{3,2,1,0:T(8,128)(2,1)}), bf16[4,2,128,256]{3,2,1,0:T(8,128)(2,1)}, u32[]{:S(2)}, u32[]{:S(2)}) %all-to-all-start.2) | async-done | bytes 524320 | tf_op jit(solution)/shard_map/all_to_all | solution.py:125
  108.5 1.6 convolution_convert_fusion.6
  111.6 2.0 reduce-scatter.3.cloned.1.call-done
  113.6 1.6 fusion.7
  115.3 1.7 fusion.3
  123.9 1.8 convolution_bitcast_fusion.1
  125.8 2.6 copy.97
  128.4 1.7 bitcast_convert_fusion
  131.5 1.8 convolution_bitcast_fusion
  133.3 2.4 copy.100
  135.7 1.8 fusion.15
  139.1 4.1 %all-to-all-start.3 = ((bf16[4,2,128,256]{3,2,1,0:T(8,128)(2,1)}), bf16[4,2,128,256]{3,2,1,0:T(8,128)(2,1)S(1)}, u32[]{:S(2)}, u32[]{:S(2)}) async-start(bf16[4,2,128,256]{3,2,1,0:T(8,128)(2,1)} %copy.102), calls=%async_computation.5 | async-start | bytes 1048576 | tf_op jit(solution)/shard_map/all_to_all | solution.py:125
  144.2 7.1 %all-to-all-done.3 = bf16[4,2,128,256]{3,2,1,0:T(8,128)(2,1)S(1)} async-done(((bf16[4,2,128,256]{3,2,1,0:T(8,128)(2,1)}), bf16[4,2,128,256]{3,2,1,0:T(8,128)(2,1)S(1)}, u32[]{:S(2)}, u32[]{:S(2)}) %all-to-all-start.3) | async-done | bytes 524320 | tf_op jit(solution)/shard_map/all_to_all | solution.py:125
  153.4 70.0 %all-reduce.3.cloned.1.call-done = (f32[2,256,512]{1,2,0:T(8,128)}, f32[2,256,512]{1,2,0:T(8,128)}, f32[2,512,256]{2,1,0:T(8,128)}) async-done(((f32[2,256,512]{1,2,0:T(8,128)}, f32[2,256,512]{1,2,0:T(8,128)}, f32[2,512,256]{2,1,0:T(8,128)}), (f32[2,256,512]{1,2,0:T(8,128)}, f32[2,256,512]{1,2,0:T(8,128)}, f32[2,512,256]{2,1,0:T(8,128)})) %all-reduce.3.cloned.1.call-update) | async-done | bytes 3145744 | tf_op jit(solution)/shard_map/psum | solution.py:141
  223.4 1.7 broadcast_multiply_fusion.1
  227.7 2.3 broadcast_multiply_fusion
  230.1 23.5 %reduce-scatter.5.cloned.1.call-done = bf16[512,256]{1,0:T(8,128)(2,1)} async-done(((bf16[2048,256]{1,0:T(8,128)(2,1)}), bf16[512,256]{1,0:T(8,128)(2,1)}) %reduce-scatter.5.cloned.1.call-update) | async-done | bytes 262160 | tf_op jit(solution)/shard_map/reduce_scatter | solution.py:107
  253.6 2.1 fusion.5
  (154 shorter events, 47.4 us)
Async XLA Ops:
  7.2 34.4 %copy-start = (bf16[4,4,128,128]{3,2,1,0:T(8,128)(2,1)S(1)}, bf16[4,4,128,128]{3,2,1,0:T(8,128)(2,1)}, u32[]{:S(2)}) copy-start(bf16[4,4,128,128]{3,2,1,0:T(8,128)(2,1)} %param.14) | copy-start | bytes 1572868
  7.2 9.7 %copy-start.10 = (bf16[512,256]{1,0:T(8,128)(2,1)S(1)}, bf16[512,256]{1,0:T(8,128)(2,1)}, u32[]{:S(2)}) copy-start(bf16[512,256]{1,0:T(8,128)(2,1)} %param.12) | copy-start | bytes 786436
  7.2 9.5 %copy-start.40 = (s32[4,4]{1,0:T(4,128)S(1)}, s32[4,4]{1,0:T(4,128)}, u32[]{:S(2)}) copy-start(s32[4,4]{1,0:T(4,128)} %param.15) | copy-start | bytes 196
  7.2 9.6 %copy-start.39 = (s32[4,4]{1,0:T(4,128)S(1)}, s32[4,4]{1,0:T(4,128)}, u32[]{:S(2)}) copy-start(s32[4,4]{1,0:T(4,128)} %param.13) | copy-start | bytes 196
  7.2 9.7 %copy-start.13 = (bf16[2,256,512]{2,1,0:T(8,128)(2,1)S(1)}, bf16[2,256,512]{2,1,0:T(8,128)(2,1)}, u32[]{:S(2)}) copy-start(bf16[2,256,512]{2,1,0:T(8,128)(2,1)} %param.20) | copy-start | bytes 1572868
  7.2 32.4 %all-gather.3.cloned.1.call-start = ((), (), s32[]{:S(2)}) async-start(), calls=%async_computation.6 | async-start | bytes 1310720 | tf_op jit(solution)/shard_map/all_gather | solution.py:47
  12.4 12.2 %all-to-all-start = ((bf16[4,2,128,256]{3,2,1,0:T(8,128)(2,1)}), bf16[4,2,128,256]{3,2,1,0:T(8,128)(2,1)S(1)}, u32[]{:S(2)}, u32[]{:S(2)}) async-start(bf16[4,2,128,256]{3,2,1,0:T(8,128)(2,1)} %copy.76), calls=%async_computation | async-start | bytes 1048576 | tf_op jit(solution)/shard_map/all_to_all | solution.py:56
  16.7 56.8 %all-gather.5.cloned.1.call-start = ((), (), s32[]{:S(2)}) async-start(), calls=%async_computation.7 | async-start | bytes 1310720 | tf_op jit(solution)/shard_map/all_gather | solution.py:47
  18.2 7.6 %copy-start.1 = (bf16[4,4,128,128]{3,2,1,0:T(8,128)(2,1)S(1)}, bf16[4,4,128,128]{3,2,1,0:T(8,128)(2,1)}, u32[]{:S(2)}) copy-start(bf16[4,4,128,128]{3,2,1,0:T(8,128)(2,1)} %param.16) | copy-start | bytes 1572868
  39.6 3.4 %copy-start.7 = (f32[512,512]{1,0:T(8,128)S(1)}, f32[512,512]{1,0:T(8,128)}, u32[]{:S(2)}) copy-start(f32[512,512]{1,0:T(8,128)} %fusion.34) | copy-start | bytes 3145732
  41.5 3.1 %copy-start.36 = (bf16[2,512,256]{2,1,0:T(8,128)(2,1)S(1)}, bf16[2,512,256]{2,1,0:T(8,128)(2,1)}, u32[]{:S(2)}) copy-start(bf16[2,512,256]{2,1,0:T(8,128)(2,1)} %param.22) | copy-start | bytes 1572868
  45.8 7.3 %copy-start.6 = (bf16[512,256]{1,0:T(8,128)(2,1)S(1)}, bf16[512,256]{1,0:T(8,128)(2,1)}, u32[]{:S(2)}) copy-start(bf16[512,256]{1,0:T(8,128)(2,1)} %fusion.12) | copy-start | bytes 786436
  45.8 7.3 %copy-start.14 = (bf16[2,256,512]{2,1,0:T(8,128)(2,1)S(1)}, bf16[2,256,512]{2,1,0:T(8,128)(2,1)}, u32[]{:S(2)}) copy-start(bf16[2,256,512]{2,1,0:T(8,128)(2,1)} %param.20) | copy-start | bytes 1572868
  48.8 12.3 %all-to-all-start.1 = ((bf16[4,2,128,256]{3,2,1,0:T(8,128)(2,1)}), bf16[4,2,128,256]{3,2,1,0:T(8,128)(2,1)S(1)}, u32[]{:S(2)}, u32[]{:S(2)}) async-start(bf16[4,2,128,256]{3,2,1,0:T(8,128)(2,1)} %copy.81), calls=%async_computation.1 | async-start | bytes 1048576 | tf_op jit(solution)/shard_map/all_to_all | solution.py:56
  53.0 60.6 %reduce-scatter.3.cloned.1.call-start = ((), (), s32[]{:S(2)}) async-start(), calls=%async_computation.8 | async-start | bytes 1310720 | tf_op jit(solution)/shard_map/reduce_scatter | solution.py:107
  93.8 6.7 %copy-start.5 = (bf16[512,512]{1,0:T(8,128)(2,1)S(1)}, bf16[512,512]{1,0:T(8,128)(2,1)}, u32[]{:S(2)}) copy-start(bf16[512,512]{1,0:T(8,128)(2,1)} %copy-done.4) | copy-start | bytes 1572868
  94.0 7.7 %copy-start.26 = (bf16[4,256,128]{1,2,0:T(8,128)(2,1)S(1)}, bf16[4,256,128]{1,2,0:T(8,128)(2,1)}, u32[]{:S(2)}) copy-start(bf16[4,256,128]{1,2,0:T(8,128)(2,1)} %copy-done.25) | copy-start | bytes 786436
  95.4 6.5 %copy-start.17 = (bf16[512,512]{1,0:T(8,128)(2,1)S(1)}, bf16[512,512]{1,0:T(8,128)(2,1)}, u32[]{:S(2)}) copy-start(bf16[512,512]{1,0:T(8,128)(2,1)} %get-tuple-element.28) | copy-start | bytes 1572868
  95.4 6.5 %copy-start.24 = (bf16[512,256]{1,0:T(8,128)(2,1)S(1)}, bf16[512,256]{1,0:T(8,128)(2,1)}, u32[]{:S(2)}) copy-start(bf16[512,256]{1,0:T(8,128)(2,1)} %param.23) | copy-start | bytes 786436
  95.4 13.1 %all-to-all-start.2 = ((bf16[4,2,128,256]{3,2,1,0:T(8,128)(2,1)}), bf16[4,2,128,256]{3,2,1,0:T(8,128)(2,1)}, u32[]{:S(2)}, u32[]{:S(2)}) async-start(bf16[4,2,128,256]{3,2,1,0:T(8,128)(2,1)} %copy.92), calls=%async_computation.3 | async-start | bytes 1048576 | tf_op jit(solution)/shard_map/all_to_all | solution.py:125
  100.5 122.9 %all-reduce.3.cloned.1.call-start = ((), (), s32[]{:S(2)}) async-start(), calls=%async_computation.10 | async-start | bytes 6291456 | tf_op jit(solution)/shard_map/psum | solution.py:141
  103.1 10.5 %copy-start.15 = (bf16[2,256,512]{2,1,0:T(8,128)(2,1)S(1)}, bf16[2,256,512]{2,1,0:T(8,128)(2,1)}, u32[]{:S(2)}) copy-start(bf16[2,256,512]{2,1,0:T(8,128)(2,1)} %param.20) | copy-start | bytes 1572868
  115.3 2.4 copy-start.19
  117.0 5.0 %copy-start.2 = (bf16[512,512]{1,0:T(8,128)(2,1)}, bf16[512,512]{1,0:T(8,128)(2,1)S(1)}, u32[]{:S(2)}) copy-start(bf16[512,512]{1,0:T(8,128)(2,1)S(1)} %fusion.3) | copy-start | bytes 1572868
  121.9 131.7 %reduce-scatter.5.cloned.1.call-start = ((), (), s32[]{:S(2)}) async-start(), calls=%async_computation.9 | async-start | bytes 1310720 | tf_op jit(solution)/shard_map/reduce_scatter | solution.py:107
  137.5 5.8 %copy-start.18 = (bf16[512,512]{1,0:T(8,128)(2,1)S(1)}, bf16[512,512]{1,0:T(8,128)(2,1)}, u32[]{:S(2)}) copy-start(bf16[512,512]{1,0:T(8,128)(2,1)} %get-tuple-element.28) | copy-start | bytes 1572868
  137.5 5.8 %copy-start.38 = (bf16[2,512,256]{2,1,0:T(8,128)(2,1)S(1)}, bf16[2,512,256]{2,1,0:T(8,128)(2,1)}, u32[]{:S(2)}) copy-start(bf16[2,512,256]{2,1,0:T(8,128)(2,1)} %param.22) | copy-start | bytes 1572868
  139.1 12.2 %all-to-all-start.3 = ((bf16[4,2,128,256]{3,2,1,0:T(8,128)(2,1)}), bf16[4,2,128,256]{3,2,1,0:T(8,128)(2,1)S(1)}, u32[]{:S(2)}, u32[]{:S(2)}) async-start(bf16[4,2,128,256]{3,2,1,0:T(8,128)(2,1)} %copy.102), calls=%async_computation.5 | async-start | bytes 1048576 | tf_op jit(solution)/shard_map/all_to_all | solution.py:125
  226.4 27.2 %copy-start.3 = (bf16[512,512]{1,0:T(8,128)(2,1)S(1)}, bf16[512,512]{1,0:T(8,128)(2,1)}, u32[]{:S(2)}) copy-start(bf16[512,512]{1,0:T(8,128)(2,1)} %copy-done.2) | copy-start | bytes 1572868
  226.4 27.2 %copy-start.12 = (f32[4,128,256]{2,1,0:T(8,128)S(1)}, f32[4,128,256]{2,1,0:T(8,128)}, u32[]{:S(2)}) copy-start(f32[4,128,256]{2,1,0:T(8,128)} %copy.105) | copy-start | bytes 1572868
  226.4 27.2 %copy-start.16 = (bf16[2,256,512]{2,1,0:T(8,128)(2,1)S(1)}, bf16[2,256,512]{2,1,0:T(8,128)(2,1)}, u32[]{:S(2)}) copy-start(bf16[2,256,512]{2,1,0:T(8,128)(2,1)} %param.20) | copy-start | bytes 1572868
  227.7 25.8 %copy-start.20 = (f32[512,256]{1,0:T(8,128)S(1)}, f32[512,256]{1,0:T(8,128)}, u32[]{:S(2)}) copy-start(f32[512,256]{1,0:T(8,128)} %copy-done.19) | copy-start | bytes 1572868
  (19 other events, 25.0 us)
Sparse Core Ops, SparseCore 0:
  9.6 29.9 all-gather.2
  46.0 27.4 all-gather.4
  87.0 26.5 reduce-scatter.2
  122.0 101.3 all-reduce.2
  225.6 27.9 reduce-scatter.4
where the time goes:
time: 264 us; the launch traced here: 262 us
  waiting for transfers between devices  145 us (55%)
  matrix products  44.8 us (17%)
  local copies, waits for them, and re-layouts  32 us (12%)
  starting transfers between devices  17.8 us (7%)
  between operations  14.4 us (5%)
  other arithmetic  7.93 us (3%)
    psum x1, waiting for transfers between devices, local(): lax.psum((stacked_self, stacked_neighbor, stacked_output), ('dom', 'sub'))  70 us
    reduce_scatter x2, waiting for transfers between devices, local(): lax.psum_scatter(jnp.einsum('mnk,nkbd->mbd', onehot, near_terms, precisio...  25.5 us
    all_gather x2, waiting for transfers between devices, local(): partition = lax.all_gather(state, 'sub', axis=0, tiled=True)  23.4 us
    all_to_all x2, waiting for transfers between devices, local(): lax.all_to_all(sendbuf, 'dom', split_axis=0, concat_axis=0, tiled=True)  13.1 us
    all_to_all x2, waiting for transfers between devices, local(): lax.all_to_all(backbuf, 'dom', split_axis=0, concat_axis=0, tiled=True)  12.5 us
    all_to_all x2, starting transfers between devices, local(): lax.all_to_all(backbuf, 'dom', split_axis=0, concat_axis=0, tiled=True)  9.16 us
    all_to_all x2, starting transfers between devices, local(): lax.all_to_all(sendbuf, 'dom', split_axis=0, concat_axis=0, tiled=True)  8.51 us
    unnamed x88, local copies, waits for them, and re-layouts  8.3 us
  transfers between devices with their start and end apart: 9, of which 9 were waited for; matrix products, arithmetic and copies ran while one was open for 20% of the time, Pallas kernels for 0%

commit v1 on v0

v1 whole, which is shorter than its diff:
```python
import functools

import jax
import jax.numpy as jnp
from jax import lax
from jax.experimental import pallas as pl
from jax.experimental.pallas import tpu as pltpu
from jax.sharding import PartitionSpec as P

F32 = jnp.float32
BF16 = jnp.bfloat16
ROWS = 16


def dot(a, b):
    return jnp.dot(a, b, preferred_element_type=F32)


def dot_nt(a, b):
    return lax.dot_general(a, b, (((1,), (1,)), ((), ())), preferred_element_type=F32)


def dot_tn(a, b):
    return lax.dot_general(a, b, (((0,), (0,)), ((), ())), preferred_element_type=F32)


def kernel(
    n_dom, n_sub, scale,
    lb, rb, sb, sc, pt,
    x_ref, lm, rm, ws, wn, wo, ct,
    upd, fg, gs, gn, go,
    adj, far, st, ag, agg, pre, hid, own,
    bsend, brecv, rsend, rrecv, rs,
    wsend, wrecv, wfull, zpart, zrecv, zfull,
    ag_s, ag_r, bf_s, bf_r, bb_s, bb_r, rs_s, rs_r,
    wd_s, wd_r, wz_s, wz_r, we_s, we_r, wf_s, wf_r,
):
    layers = ws.shape[0]
    nb, blk = lm.shape[0], lm.shape[2]
    width = x_ref.shape[1]
    rounds, slots = sb.shape[1], sb.shape[2]
    here = nb * blk
    chunks = ag_r.shape[2]
    crow = here // chunks
    dom = lax.axis_index("dom")
    sub = lax.axis_index("sub")
    pending = []

    def remote(src, dst, send, recv, axis, peer):
        return pltpu.make_async_remote_copy(
            src_ref=src, dst_ref=dst, send_sem=send, recv_sem=recv,
            device_id={axis: peer}, device_id_type=pl.DeviceIdType.MESH,
        )

    def start(copy, cond=None):
        if cond is None:
            copy.start()
        else:
            pl.when(cond)(copy.start)
        pending.append((copy, cond))

    barrier = pltpu.get_barrier_semaphore()
    for axis, me, n in (("dom", dom, n_dom), ("sub", sub, n_sub)):
        for d in range(1, n):
            pl.semaphore_signal(
                barrier, inc=1, device_id={axis: lax.rem(me + d, n)},
                device_id_type=pl.DeviceIdType.MESH,
            )
    pl.semaphore_wait(barrier, n_dom + n_sub - 2)

    right, left = jnp.minimum(sub + 1, n_sub - 1), jnp.maximum(sub - 1, 0)
    has_right, has_left = sub < n_sub - 1, sub > 0

    def gather_start(l):
        for c in range(chunks):
            part = st.at[l, pl.ds(c * crow, crow)]
            there = ag.at[l, sub, pl.ds(c * crow, crow)]
            start(remote(part, there, ag_s.at[l, sub, c, 0], ag_r.at[l, sub, c], "sub", right), has_right)
            start(remote(part, there, ag_s.at[l, sub, c, 1], ag_r.at[l, sub, c], "sub", left), has_left)

    def gather_step(l, d):
        for c in range(chunks):
            for src, ok, to, more, way in (
                (sub - d, sub - d >= 0, right, has_right, 0),
                (sub + d, sub + d < n_sub, left, has_left, 1),
            ):
                at = jnp.clip(src, 0, n_sub - 1)
                part = ag.at[l, at, pl.ds(c * crow, crow)]
                copy = remote(part, part, ag_s.at[l, at, c, way], ag_r.at[l, at, c], "sub", to)
                pl.when(ok)(copy.wait_recv)
                start(copy, jnp.logical_and(ok, more))

    def picks(p, j):
        out = []
        for b in range(nb):
            one = jnp.float32(0.0)
            for r in range(rounds):
                good = (pt[r, dom] == p) & (j < sc[0, r]) & (sb[0, r, j] == b)
                one = one + jnp.where(good, 1.0, 0.0)
            out.append(one)
        return out

    def boundary_start(l):
        for d in range(1, n_dom):
            p = lax.rem(dom + d, n_dom)
            for j in range(slots):
                ones = picks(p, j)
                total = jnp.zeros((blk, width), F32)
                for b in range(nb):
                    total = total + st[l, b * blk:(b + 1) * blk, :].astype(F32) * ones[b]
                bsend[l, p, j * blk:(j + 1) * blk, :] = total.astype(BF16)
            start(remote(bsend.at[l, p], brecv.at[l, dom], bf_s.at[l, p], bf_r.at[l, dom], "dom", p))

    def arrive(buf, sems, l, axis, me, n):
        for d in range(1, n):
            src = lax.rem(me + n - d, n)
            remote(buf.at[l, src], buf.at[l, src], sems.at[l, src], sems.at[l, src], axis, src).wait_recv()

    def build(matrix, column, out, count):
        @pl.loop(0, count)
        def _(t):
            at = pl.multiple_of(t * blk, blk)
            for b in range(nb):
                total = jnp.zeros((blk, blk), F32)
                for k in range(matrix.shape[1]):
                    hit = jnp.where(column(b, k) == t, 1.0, 0.0)
                    total = total + matrix[b, k].astype(F32) * hit
                out[b * blk:(b + 1) * blk, pl.ds(at, blk)] = total.astype(BF16)

    def far_column(b, k):
        slot = rb[b, k]
        r = lax.div(slot, slots)
        return pt[r, dom] * slots + (slot - r * slots)

    st[0] = x_ref[...]
    for l in range(layers):
        gather_start(l)
        boundary_start(l)
        ag[l, sub] = st[l]
        brecv[l, dom] = jnp.zeros(brecv.shape[2:], BF16)
        if l == 0:
            build(lm, lambda b, k: lb[b, k], adj, n_sub * nb)
            build(rm, far_column, far, n_dom * slots)
        gather_step(l, 1)
        pre[l] = dot(st[l], ws[l])
        arrive(brecv, bf_r, l, "dom", dom, n_dom)
        total = dot(far[...], brecv[l].reshape(-1, width))
        for d in range(2, n_sub):
            gather_step(l, d)
        total = total + dot(adj[...], ag[l].reshape(-1, width))
        agg[l] = total.astype(BF16)
        preact = pre[l] + dot(agg[l], wn[l])
        pre[l] = preact
        hid[l] = (preact / (1.0 + jnp.exp(-preact))).astype(BF16)
        result = (st[l].astype(F32) + dot(hid[l], wo[l])).astype(BF16)
        if l + 1 < layers:
            st[l + 1] = result
        else:
            upd[...] = result

    wrows = wsend.shape[2]
    zrows = zpart.shape[2]

    def weights_start(l, cot, gp):
        tall = jnp.concatenate(
            [dot_tn(st[l], gp), dot_tn(agg[l], gp), dot_tn(cot, hid[l])], axis=0
        ).astype(BF16)
        for p in range(n_dom):
            wsend[l, p] = tall[p * wrows:(p + 1) * wrows]
        for d in range(1, n_dom):
            p = lax.rem(dom + d, n_dom)
            start(remote(wsend.at[l, p], wrecv.at[l, dom], wd_s.at[l, p], wd_r.at[l, dom], "dom", p))

    def weights_dom(l):
        arrive(wrecv, wd_r, l, "dom", dom, n_dom)
        total = wsend[l, dom].astype(F32)
        for d in range(1, n_dom):
            total = total + wrecv[l, lax.rem(dom + d, n_dom)].astype(F32)
        total = total.astype(BF16)
        for s in range(n_sub):
            low, high = min(s * zrows, wrows), min((s + 1) * zrows, wrows)
            if high > low:
                zpart[l, s, :high - low] = total[low:high]
            if high - low < zrows:
                zpart[l, s, high - low:] = jnp.zeros((zrows - high + low, total.shape[1]), BF16)
        for d in range(1, n_sub):
            s = lax.rem(sub + d, n_sub)
            start(remote(zpart.at[l, s], zrecv.at[l, sub], wz_s.at[l, s], wz_r.at[l, sub], "sub", s))

    def weights_sub(l):
        arrive(zrecv, wz_r, l, "sub", sub, n_sub)
        total = zpart[l, sub].astype(F32)
        for d in range(1, n_sub):
            total = total + zrecv[l, lax.rem(sub + d, n_sub)].astype(F32)
        zfull[l, sub] = total.astype(BF16)
        for d in range(1, n_sub):
            s = lax.rem(sub + d, n_sub)
            start(remote(zfull.at[l, sub], zfull.at[l, sub], we_s.at[l, s], we_r.at[l, sub], "sub", s))

    def weights_back(l):
        arrive(zfull, we_r, l, "sub", sub, n_sub)
        wfull[l, dom] = zfull[l].reshape(n_sub * zrows, -1)[:wrows]
        for d in range(1, n_dom):
            p = lax.rem(dom + d, n_dom)
            start(remote(wfull.at[l, dom], wfull.at[l, dom], wf_s.at[l, p], wf_r.at[l, dom], "dom", p))

    def weights_done(l):
        arrive(wfull, wf_r, l, "dom", dom, n_dom)
        tall = wfull[l].reshape(n_dom * wrows, -1).astype(F32) * scale
        gs[l] = tall[:width]
        gn[l] = tall[width:2 * width]
        go[l] = tall[2 * width:].T

    def reduce_start(l, ga):
        for d in range(n_sub - 1, -1, -1):
            for way in (0, 1) if d else (0,):
                raw = sub - d if way else sub + d
                ok = raw >= 0 if way else raw < n_sub
                t = jnp.clip(raw, 0, n_sub - 1)

                @pl.when(ok)
                def _(t=t):
                    own[t] = dot_tn(adj[:, pl.ds(pl.multiple_of(t * here, here), here)], ga)

                if d:
                    edge = sub == (n_sub - 1 if way else 0)
                    reduce_send(l, t, way, jnp.logical_and(ok, edge), False)

    def reduce_send(l, t, way, cond, add):
        to = left if way else right
        for c in range(chunks):
            rows = pl.ds(c * crow, crow)
            part = rs.at[l, t, rows]
            land = jnp.where(t == to, n_sub, t) if way else t
            copy = remote(part, rs.at[l, land, rows], rs_s.at[l, t, c], rs_r.at[l, land, c], "sub", to)

            @pl.when(cond)
            def _(t=t, rows=rows, part=part, c=c):
                value = own[t, rows]
                if add:
                    remote(part, part, rs_s.at[l, t, c], rs_r.at[l, t, c], "sub", to).wait_recv()
                    value = value + rs[l, t, rows].astype(F32)
                rs[l, t, rows] = value.astype(BF16)

            start(copy, cond)

    def reduce_finish(l):
        for d in range(n_sub - 1, 0, -1):
            for way in (0, 1):
                raw = sub - d if way else sub + d
                ok = raw >= 0 if way else raw < n_sub
                inner = has_right if way else has_left
                reduce_send(l, jnp.clip(raw, 0, n_sub - 1), way, jnp.logical_and(ok, inner), True)

    def reduce_last(l):
        for cond, slot in ((has_left, sub), (has_right, n_sub)):
            @pl.when(cond)
            def _(slot=slot):
                for c in range(chunks):
                    rows = pl.ds(c * crow, crow)
                    part = rs.at[l, slot, rows]
                    remote(part, part, rs_r.at[l, slot, c], rs_r.at[l, slot, c], "sub", left).wait_recv()
                    own[sub, rows] += rs[l, slot, rows].astype(F32)
        return own[sub]

    fg[...] = ct[...].astype(F32)
    for l in range(layers - 1, -1, -1):
        cot = fg[...].astype(BF16)
        preact = pre[l]
        logistic = 1.0 / (1.0 + jnp.exp(-preact))
        gp = (dot_nt(cot, wo[l]) * logistic * (1.0 + preact * (1.0 - logistic))).astype(BF16)
        ga = dot_nt(gp, wn[l]).astype(BF16)
        reduce_start(l, ga)
        rsend[l] = dot_tn(far[...], ga).astype(BF16).reshape(rsend.shape[1:])
        for d in range(1, n_dom):
            p = lax.rem(dom + d, n_dom)
            start(remote(rsend.at[l, p], rrecv.at[l, dom], bb_s.at[l, p], bb_r.at[l, dom], "dom", p))
        weights_start(l, cot, gp)
        if l + 1 < layers:
            weights_dom(l + 1)
        upstream = fg[...] + dot_nt(gp, ws[l])
        reduce_finish(l)
        if l + 1 < layers:
            weights_sub(l + 1)
        fg[...] = upstream
        arrive(rrecv, bb_r, l, "dom", dom, n_dom)
        for d in range(1, n_dom):
            p = lax.rem(dom + d, n_dom)
            for j in range(slots):
                ones = picks(p, j)
                slot = rrecv[l, p, j * blk:(j + 1) * blk, :].astype(F32)
                for b in range(nb):
                    fg[b * blk:(b + 1) * blk, :] += slot * ones[b]
        if l == 0:
            weights_dom(l)
        near = reduce_last(l)
        fg[...] = fg[...] + near
        if l + 1 < layers:
            weights_back(l + 1)
    weights_sub(0)
    for l in range(layers - 1, 0, -1):
        weights_done(l)
    weights_back(0)
    weights_done(0)
    for copy, cond in pending:
        if cond is None:
            copy.wait_send()
        else:
            pl.when(cond)(copy.wait_send)


def local(features, local_blocks, local_matrix, remote_blocks, remote_matrix, send_blocks,
          send_counts, partner, self_weight, neighbor_weight, output_weight, output_cotangent):
    n_dom, n_sub = lax.axis_size("dom"), lax.axis_size("sub")
    layers, width, units = self_weight.shape
    here = features.shape[0]
    nb, blk = local_matrix.shape[0], local_matrix.shape[2]
    slots = send_blocks.shape[2]
    scale = 1.0 / (here * n_dom * n_sub) ** 0.5
    chunks = 2
    wrows = 3 * width // n_dom
    zrows = -(-wrows // (n_sub * ROWS)) * ROWS
    vmem, smem = pl.BlockSpec(memory_space=pltpu.VMEM), pl.BlockSpec(memory_space=pltpu.SMEM)
    dma = pltpu.SemaphoreType.DMA
    edge = (layers, n_dom, slots * blk, width)
    tall = (layers, n_dom, wrows, units)
    small = (layers, n_sub, zrows, units)
    return pl.pallas_call(
        functools.partial(kernel, n_dom, n_sub, scale),
        out_shape=(
            jax.ShapeDtypeStruct((here, width), BF16),
            jax.ShapeDtypeStruct((here, width), F32),
            jax.ShapeDtypeStruct((layers, width, units), F32),
            jax.ShapeDtypeStruct((layers, width, units), F32),
            jax.ShapeDtypeStruct((layers, units, width), F32),
        ),
        in_specs=[smem] * 5 + [vmem] * 7,
        out_specs=(vmem,) * 5,
        scratch_shapes=[
            pltpu.VMEM((here, n_sub * here), BF16),
            pltpu.VMEM((here, n_dom * slots * blk), BF16),
            pltpu.VMEM((layers, here, width), BF16),
            pltpu.VMEM((layers, n_sub, here, width), BF16),
            pltpu.VMEM((layers, here, width), BF16),
            pltpu.VMEM((layers, here, units), F32),
            pltpu.VMEM((layers, here, units), BF16),
            pltpu.VMEM((n_sub, here, width), F32),
            pltpu.VMEM(edge, BF16),
            pltpu.VMEM(edge, BF16),
            pltpu.VMEM(edge, BF16),
            pltpu.VMEM(edge, BF16),
            pltpu.VMEM((layers, n_sub + 1, here, width), BF16),
            pltpu.VMEM(tall, BF16),
            pltpu.VMEM(tall, BF16),
            pltpu.VMEM(tall, BF16),
            pltpu.VMEM(small, BF16),
            pltpu.VMEM(small, BF16),
            pltpu.VMEM(small, BF16),
            dma((layers, n_sub, chunks, 2)),
            dma((layers, n_sub, chunks)),
            dma((layers, n_dom)),
            dma((layers, n_dom)),
            dma((layers, n_dom)),
            dma((layers, n_dom)),
            dma((layers, n_sub, chunks)),
            dma((layers, n_sub + 1, chunks)),
            dma((layers, n_dom)),
            dma((layers, n_dom)),
            dma((layers, n_sub)),
            dma((layers, n_sub)),
            dma((layers, n_sub)),
            dma((layers, n_sub)),
            dma((layers, n_dom)),
            dma((layers, n_dom)),
        ],
        compiler_params=pltpu.CompilerParams(
            collective_id=0, has_side_effects=True, vmem_limit_bytes=60 * 1024 * 1024
        ),
    )(local_blocks, remote_blocks, send_blocks, send_counts, partner, features, local_matrix,
      remote_matrix, self_weight, neighbor_weight, output_weight, output_cotangent)


def solution(mesh):
    whole = ("region", "dom", "sub")
    in_specs = (
        P(whole, None), P(whole, None), P(whole, None, None, None), P(whole, None),
        P(whole, None, None, None), P(whole, None, None), P(whole, None), P("region", None),
        P(), P(), P(), P(whole, None),
    )
    out_specs = (
        P(whole, None), P(whole, None), P("region", None, None), P("region", None, None),
        P("region", None, None),
    )
    return jax.shard_map(local, mesh=mesh, in_specs=in_specs, out_specs=out_specs, check_vma=False)
```

time: 264 us -> 119 us (0.45)
  waiting for transfers between devices: 145 us -> 0 us
  Pallas kernels: 0 us -> 110 us
  matrix products: 44.8 us -> 0 us
  local copies, waits for them, and re-layouts: 32 us -> 7.8 us
  starting transfers between devices: 17.8 us -> 0 us
  between operations: 14.4 us -> 0.66 us
  other arithmetic: 7.93 us -> 0 us
    pallas_call x0 -> x1, Pallas kernels: none -> 110 us  [local(): pl.pallas_call(functools.partial(kernel, n_dom, n_sub, scale), out_shape=...]
    psum x1 -> x0, waiting for transfers between devices: 70 us -> none  [local(): lax.psum((stacked_self, stacked_neighbor, stacked_output), ('dom', 'sub'))]
    dot_general x42 -> x0, matrix products: 44.8 us -> none  [the longest x2 5.11 us: local(): jnp.einsum('qnk,nkbd->qbd', slot_onehot, far_terms, precision=lax.Precisi...]
    all_to_all x4 -> x0, waiting for transfers between devices: 25.6 us -> none  [the longest x2 13.1 us: local(): lax.all_to_all(sendbuf, 'dom', split_axis=0, concat_axis=0, tiled=True)]
    reduce_scatter x2 -> x0, waiting for transfers between devices: 25.5 us -> none  [local(): lax.psum_scatter(jnp.einsum('mnk,nkbd->mbd', onehot, near_terms, precisio...]
    all_gather x2 -> x0, waiting for transfers between devices: 23.4 us -> none  [local(): partition = lax.all_gather(state, 'sub', axis=0, tiled=True)]
    all_to_all x4 -> x0, starting transfers between devices: 17.7 us -> none  [the longest x2 9.16 us: local(): lax.all_to_all(backbuf, 'dom', split_axis=0, concat_axis=0, tiled=True)]
    dot_general x6 -> x0, local copies, waits for them, and re-layouts: 11.2 us -> none  [the longest x2 4.97 us: local(): jnp.einsum('nkab,nad->nkbd', local_matrix, grad_blocks, preferred_element...]
  transfers between devices with their start and end apart: 9 -> 0, of which waited for: 9 -> 0; matrix products, arithmetic and copies ran while one was open for 20% -> 0% of each run, Pallas kernels for 0% -> 0%
where the time goes in v1:
time: 119 us
  Pallas kernels  110 us (92%)
  local copies, waits for them, and re-layouts  7.8 us (7%)
    pallas_call x1, Pallas kernels, local(): pl.pallas_call(functools.partial(kernel, n_dom, n_sub, scale), out_shape=...  110 us
    unnamed x11, local copies, waits for them, and re-layouts  7.8 us

profile of v1, /device:TPU:1, one launch (start us, length us, event | category | flops | bytes accessed | tf_op | source)
XLA Modules:
  0.0 118.7 jit_solution(10995632557468420174)
XLA Ops:
  0.6 110.2 %shard_map.155 = (bf16[512,256]{1,0:T(8,128)(2,1)}, f32[512,256]{1,0:T(8,128)}, f32[2,256,512]{2,1,0:T(8,128)}, f32[2,256,512]{2,1,0:T(8,128)}, f32[2,512,256]{2,1,0:T(8,128)}) custom-call(s32[4,4]{1,0:T(4,128)} %lb.1, s32[4,4]{1,0:T(4,128)} %rb.1, s32[1,2,2]{2,1,0:T(2,128)} %sb.1, s32[1,2]{1,0:T(1,128)} %sc.1, s32[2,4]{1,0:T(2,128)} %pt.1, ...), custom_call_target="tpu_custom_call" | custom-call | tf_op jit(solution)/shard_map/pallas_call | solution.py:328
  110.9 0.0 copy-start.2
  110.9 1.8 %copy.22 = bf16[512,256]{1,0:T(8,128)(2,1)} copy(bf16[512,256]{1,0:T(8,128)(2,1)} %get-tuple-element.10) | data formatting | bytes 524288
  112.6 1.9 %copy.23 = f32[512,256]{1,0:T(8,128)} copy(f32[512,256]{1,0:T(8,128)} %get-tuple-element.11) | data formatting | bytes 1048576
  114.5 0.0 copy-done.2
  114.5 0.0 copy-start.1
  114.5 1.0 copy.24
  115.5 0.6 copy-done.1
  116.1 0.0 copy-start
  116.1 1.0 copy.25
  117.1 0.6 copy-done
  117.7 1.0 copy.26
Async XLA Ops:
  110.9 3.6 %copy-start.2 = (f32[2,256,512]{2,1,0:T(8,128)S(1)}, f32[2,256,512]{2,1,0:T(8,128)}, u32[]{:S(2)}) copy-start(f32[2,256,512]{2,1,0:T(8,128)} %get-tuple-element.12) | copy-start | bytes 3145732
  114.5 1.6 %copy-start.1 = (f32[2,256,512]{2,1,0:T(8,128)S(1)}, f32[2,256,512]{2,1,0:T(8,128)}, u32[]{:S(2)}) copy-start(f32[2,256,512]{2,1,0:T(8,128)} %get-tuple-element.13) | copy-start | bytes 3145732
  116.1 1.6 %copy-start = (f32[2,512,256]{2,1,0:T(8,128)S(1)}, f32[2,512,256]{2,1,0:T(8,128)}, u32[]{:S(2)}) copy-start(f32[2,512,256]{2,1,0:T(8,128)} %get-tuple-element.14) | copy-start | bytes 3145732

commit v2 on v1

--- a/solution.py
+++ b/solution.py
@@ -25,15 +25,16 @@
 
 
 def kernel(
-    n_dom, n_sub, scale,
+    n_dom, n_sub,
     lb, rb, sb, sc, pt,
-    x_ref, lm, rm, ws, wn, wo, ct,
-    upd, fg, gs, gn, go,
+    x_ref, lm_h, rm_h, ws_h, wn_h, wo_h, ct_h,
+    upd, fg, wfull,
+    lm, rm, ws, wn, wo, ct, in_sem,
     adj, far, st, ag, agg, pre, hid, own,
     bsend, brecv, rsend, rrecv, rs,
-    wsend, wrecv, wfull, zpart, zrecv, zfull,
+    wpart, crecv, xsend, xrecv, zpart, zrecv,
     ag_s, ag_r, bf_s, bf_r, bb_s, bb_r, rs_s, rs_r,
-    wd_s, wd_r, wz_s, wz_r, we_s, we_r, wf_s, wf_r,
+    wc_s, wc_r, wx_s, wx_r, wz_s, wz_r, we_s, we_r, wf_s, wf_r, wm_s, wm_r,
 ):
     layers = ws.shape[0]
     nb, blk = lm.shape[0], lm.shape[2]
@@ -59,6 +60,14 @@
             pl.when(cond)(copy.start)
         pending.append((copy, cond))
 
+    loads = {}
+    for i, (name, src, dst) in enumerate((
+        ("lm", lm_h, lm), ("rm", rm_h, rm), ("ws", ws_h, ws),
+        ("wn", wn_h, wn), ("wo", wo_h, wo), ("ct", ct_h, ct),
+    )):
+        loads[name] = pltpu.make_async_copy(src, dst, in_sem.at[i])
+        loads[name].start()
+
     barrier = pltpu.get_barrier_semaphore()
     for axis, me, n in (("dom", dom, n_dom), ("sub", sub, n_sub)):
         for d in range(1, n):
@@ -78,8 +87,8 @@
             start(remote(part, there, ag_s.at[l, sub, c, 0], ag_r.at[l, sub, c], "sub", right), has_right)
             start(remote(part, there, ag_s.at[l, sub, c, 1], ag_r.at[l, sub, c], "sub", left), has_left)
 
-    def gather_step(l, d):
-        for c in range(chunks):
+    def gather_step(l, d, c):
+        for _ in (0,):
             for src, ok, to, more, way in (
                 (sub - d, sub - d >= 0, right, has_right, 0),
                 (sub + d, sub + d < n_sub, left, has_left, 1),
@@ -116,8 +125,8 @@
             src = lax.rem(me + n - d, n)
             remote(buf.at[l, src], buf.at[l, src], sems.at[l, src], sems.at[l, src], axis, src).wait_recv()
 
-    def build(matrix, column, out, count):
-        @pl.loop(0, count)
+    def build(matrix, column, out, low, count):
+        @pl.loop(low, count)
         def _(t):
             at = pl.multiple_of(t * blk, blk)
             for b in range(nb):
@@ -132,23 +141,52 @@
         r = lax.div(slot, slots)
         return pt[r, dom] * slots + (slot - r * slots)
 
+    def local_column(b, k):
+        return lb[b, k]
+
+    def gathered(l, d):
+        for raw in (sub - d, sub + d):
+            @pl.when(jnp.logical_and(raw >= 0, raw < n_sub))
+            def _(at=jnp.clip(raw, 0, n_sub - 1)):
+                cols = pl.ds(pl.multiple_of(at * here, here), here)
+                own[0] += dot(adj[:, cols], ag[l, at])
+
     st[0] = x_ref[...]
     for l in range(layers):
         gather_start(l)
         boundary_start(l)
-        ag[l, sub] = st[l]
         brecv[l, dom] = jnp.zeros(brecv.shape[2:], BF16)
         if l == 0:
-            build(lm, lambda b, k: lb[b, k], adj, n_sub * nb)
-            build(rm, far_column, far, n_dom * slots)
-        gather_step(l, 1)
-        pre[l] = dot(st[l], ws[l])
-        arrive(brecv, bf_r, l, "dom", dom, n_dom)
-        total = dot(far[...], brecv[l].reshape(-1, width))
+            half = n_sub * nb // 2
+            loads["lm"].wait()
+            build(lm, local_column, adj, 0, half)
+            gather_step(l, 1, 0)
+            build(lm, local_column, adj, half, 2 * half)
+            for c in range(1, chunks):
+                gather_step(l, 1, c)
+            loads["rm"].wait()
+            build(rm, far_column, far, 0, n_dom * slots)
+            loads["ws"].wait()
+            pre[l] = dot(st[l], ws[l])
+        else:
+            pre[l] = dot(st[l], ws[l])
+            for c in range(chunks):
+                gather_step(l, 1, c)
+        own[0] = dot(adj[:, pl.ds(pl.multiple_of(sub * here, here), here)], st[l])
         for d in range(2, n_sub):
-            gather_step(l, d)
-        total = total + dot(adj[...], ag[l].reshape(-1, width))
-        agg[l] = total.astype(BF16)
+            for c in range(chunks):
+                gather_step(l, d, c)
+                if c == 0:
+                    gathered(l, d - 1)
+            if d == 2:
+                arrive(brecv, bf_r, l, "dom", dom, n_dom)
+                own[0] += dot(far[...], brecv[l].reshape(-1, width))
+        gathered(l, n_sub - 1)
+        if l == 0:
+            loads["wn"].wait()
+            loads["wo"].wait()
+            loads["ct"].wait()
+        agg[l] = own[0].astype(BF16)
         preact = pre[l] + dot(agg[l], wn[l])
         pre[l] = preact
         hid[l] = (preact / (1.0 + jnp.exp(-preact))).astype(BF16)
@@ -158,24 +196,36 @@
         else:
             upd[...] = result
 
-    wrows = wsend.shape[2]
+    wrows = xsend.shape[2]
     zrows = zpart.shape[2]
+    pairs = n_dom // 2
+    pair, side = lax.div(dom, 2), lax.rem(dom, 2)
+    mate = dom + 1 - 2 * side
 
     def weights_start(l, cot, gp):
+        out = dot_tn(hid[l], cot)
         tall = jnp.concatenate(
-            [dot_tn(st[l], gp), dot_tn(agg[l], gp), dot_tn(cot, hid[l])], axis=0
-        ).astype(BF16)
+            [dot_tn(st[l], gp), dot_tn(agg[l], gp),
+             jnp.concatenate([out[i:i + width] for i in range(0, out.shape[0], width)], axis=1)],
+            axis=0,
+        )
         for p in range(n_dom):
-            wsend[l, p] = tall[p * wrows:(p + 1) * wrows]
-        for d in range(1, n_dom):
-            p = lax.rem(dom + d, n_dom)
-            start(remote(wsend.at[l, p], wrecv.at[l, dom], wd_s.at[l, p], wd_r.at[l, dom], "dom", p))
+            wpart[l, p % 2, p // 2] = tall[p * wrows:(p + 1) * wrows]
+        start(remote(wpart.at[l, 1 - side], crecv.at[l], wc_s.at[l], wc_r.at[l], "dom", mate))
+
+    def weights_pair(l):
+        remote(crecv.at[l], crecv.at[l], wc_s.at[l], wc_r.at[l], "dom", mate).wait_recv()
+        for d in range(1, pairs):
+            q = lax.rem(pair + d, pairs)
+            xsend[l, q] = (wpart[l, side, q] + crecv[l, q]).astype(BF16)
+            start(remote(xsend.at[l, q], xrecv.at[l, pair], wx_s.at[l, q], wx_r.at[l, pair], "dom", 2 * q + side))
 
     def weights_dom(l):
-        arrive(wrecv, wd_r, l, "dom", dom, n_dom)
-        total = wsend[l, dom].astype(F32)
-        for d in range(1, n_dom):
-            total = total + wrecv[l, lax.rem(dom + d, n_dom)].astype(F32)
+        total = wpart[l, side, pair] + crecv[l, pair]
+        for d in range(1, pairs):
+            q = lax.rem(pair + pairs - d, pairs)
+            remote(xrecv.at[l, q], xrecv.at[l, q], wx_s.at[l, q], wx_r.at[l, q], "dom", mate).wait_recv()
+            total = total + xrecv[l, q].astype(F32)
         total = total.astype(BF16)
         for s in range(n_sub):
             low, high = min(s * zrows, wrows), min((s + 1) * zrows, wrows)
@@ -187,29 +237,47 @@
             s = lax.rem(sub + d, n_sub)
             start(remote(zpart.at[l, s], zrecv.at[l, sub], wz_s.at[l, s], wz_r.at[l, sub], "sub", s))
 
+    def spread(l, s):
+        part = wfull.at[l, dom, s]
+        start(remote(part, part, wm_s.at[l, pair, s], wm_r.at[l, dom, s], "dom", mate))
+        for d in range(1, pairs):
+            q = lax.rem(pair + d, pairs)
+            start(remote(part, part, wf_s.at[l, q, s], wf_r.at[l, pair, s], "dom", 2 * q + side))
+
     def weights_sub(l):
         arrive(zrecv, wz_r, l, "sub", sub, n_sub)
         total = zpart[l, sub].astype(F32)
         for d in range(1, n_sub):
             total = total + zrecv[l, lax.rem(sub + d, n_sub)].astype(F32)
-        zfull[l, sub] = total.astype(BF16)
+        wfull[l, dom, sub] = total.astype(BF16)
+        part = wfull.at[l, dom, sub]
         for d in range(1, n_sub):
             s = lax.rem(sub + d, n_sub)
-            start(remote(zfull.at[l, sub], zfull.at[l, sub], we_s.at[l, s], we_r.at[l, sub], "sub", s))
+            start(remote(part, part, we_s.at[l, s], we_r.at[l, sub], "sub", s))
+        spread(l, sub)
 
     def weights_back(l):
-        arrive(zfull, we_r, l, "sub", sub, n_sub)
-        wfull[l, dom] = zfull[l].reshape(n_sub * zrows, -1)[:wrows]
-        for d in range(1, n_dom):
-            p = lax.rem(dom + d, n_dom)
-            start(remote(wfull.at[l, dom], wfull.at[l, dom], wf_s.at[l, p], wf_r.at[l, dom], "dom", p))
+        for d in range(1, n_sub):
+            s = lax.rem(sub + n_sub - d, n_sub)
+            part = wfull.at[l, dom, s]
+            remote(part, part, we_s.at[l, s], we_r.at[l, s], "sub", s).wait_recv()
+            spread(l, s)
+
+    def weights_pass(l):
+        for k in range(n_sub):
+            s = lax.rem(sub + n_sub - k, n_sub)
+            for d in range(1, pairs):
+                q = lax.rem(pair + pairs - d, pairs)
+                part = wfull.at[l, 2 * q + side, s]
+                remote(part, part, wf_s.at[l, q, s], wf_r.at[l, q, s], "dom", mate).wait_recv()
+                start(remote(part, part, wm_s.at[l, q, s], wm_r.at[l, 2 * q + side, s], "dom", mate))
 
     def weights_done(l):
-        arrive(wfull, wf_r, l, "dom", dom, n_dom)
-        tall = wfull[l].reshape(n_dom * wrows, -1).astype(F32) * scale
-        gs[l] = tall[:width]
-        gn[l] = tall[width:2 * width]
-        go[l] = tall[2 * width:].T
+        for s in range(n_sub):
+            for q in range(pairs):
+                p = 2 * q + 1 - side
+                part = wfull.at[l, p, s]
+                remote(part, part, wm_s.at[l, q, s], wm_r.at[l, p, s], "dom", mate).wait_recv()
 
     def reduce_start(l, ga):
         for d in range(n_sub - 1, -1, -1):
@@ -277,12 +345,12 @@
             start(remote(rsend.at[l, p], rrecv.at[l, dom], bb_s.at[l, p], bb_r.at[l, dom], "dom", p))
         weights_start(l, cot, gp)
         if l + 1 < layers:
-            weights_dom(l + 1)
+            weights_sub(l + 1)
         upstream = fg[...] + dot_nt(gp, ws[l])
+        weights_pair(l)
         reduce_finish(l)
-        if l + 1 < layers:
-            weights_sub(l + 1)
         fg[...] = upstream
+        weights_dom(l)
         arrive(rrecv, bb_r, l, "dom", dom, n_dom)
         for d in range(1, n_dom):
             p = lax.rem(dom + d, n_dom)
@@ -291,22 +359,44 @@
                 slot = rrecv[l, p, j * blk:(j + 1) * blk, :].astype(F32)
                 for b in range(nb):
                     fg[b * blk:(b + 1) * blk, :] += slot * ones[b]
-        if l == 0:
-            weights_dom(l)
         near = reduce_last(l)
         fg[...] = fg[...] + near
-        if l + 1 < layers:
-            weights_back(l + 1)
+    for l in range(layers - 1, 0, -1):
+        weights_back(l)
     weights_sub(0)
     for l in range(layers - 1, 0, -1):
+        weights_pass(l)
+    weights_back(0)
+    weights_pass(0)
+    for l in range(layers):
         weights_done(l)
-    weights_back(0)
-    weights_done(0)
     for copy, cond in pending:
         if cond is None:
             copy.wait_send()
         else:
             pl.when(cond)(copy.wait_send)
+
+
+def finish(scale, wrows, u_ref, f_ref, w_ref, upd, fg, gs, gn, go):
+    upd[...] = u_ref[...]
+    fg[...] = f_ref[...]
+    n_dom, n_sub, zrows, units = w_ref.shape[1:]
+    width = gs.shape[1]
+    tall = w_ref[0].reshape(n_dom, n_sub * zrows, units)
+    for p in range(n_dom):
+        low = p * wrows
+        while low < (p + 1) * wrows:
+            high = min((p + 1) * wrows, (low // width + 1) * width)
+            part = tall[p, low - p * wrows:high - p * wrows].astype(F32) * scale
+            at = low % width
+            if low < width:
+                gs[0, at:at + high - low] = part
+            elif low < 2 * width:
+                gn[0, at:at + high - low] = part
+            else:
+                for i in range(0, units, width):
+                    go[0, i + at:i + at + high - low] = part[:, i:i + width]
+            low = high
 
 
 def local(features, local_blocks, local_matrix, remote_blocks, remote_matrix, send_blocks,
@@ -323,20 +413,27 @@
     vmem, smem = pl.BlockSpec(memory_space=pltpu.VMEM), pl.BlockSpec(memory_space=pltpu.SMEM)
     dma = pltpu.SemaphoreType.DMA
     edge = (layers, n_dom, slots * blk, width)
-    tall = (layers, n_dom, wrows, units)
+    half = (layers, n_dom // 2, wrows, units)
     small = (layers, n_sub, zrows, units)
-    return pl.pallas_call(
-        functools.partial(kernel, n_dom, n_sub, scale),
+    full = (layers, n_dom, n_sub, zrows, units)
+    anywhere = pl.BlockSpec(memory_space=pl.ANY)
+    upd, fg, weights = pl.pallas_call(
+        functools.partial(kernel, n_dom, n_sub),
         out_shape=(
             jax.ShapeDtypeStruct((here, width), BF16),
             jax.ShapeDtypeStruct((here, width), F32),
-            jax.ShapeDtypeStruct((layers, width, units), F32),
-            jax.ShapeDtypeStruct((layers, width, units), F32),
-            jax.ShapeDtypeStruct((layers, units, width), F32),
+            jax.ShapeDtypeStruct(full, BF16),
         ),
-        in_specs=[smem] * 5 + [vmem] * 7,
-        out_specs=(vmem,) * 5,
+        in_specs=[smem] * 5 + [vmem] + [anywhere] * 6,
+        out_specs=(vmem,) * 3,
         scratch_shapes=[
+            pltpu.VMEM(local_matrix.shape, BF16),
+            pltpu.VMEM(remote_matrix.shape, BF16),
+            pltpu.VMEM(self_weight.shape, BF16),
+            pltpu.VMEM(neighbor_weight.shape, BF16),
+            pltpu.VMEM(output_weight.shape, BF16),
+            pltpu.VMEM(output_cotangent.shape, BF16),
+            dma((6,)),
             pltpu.VMEM((here, n_sub * here), BF16),
             pltpu.VMEM((here, n_dom * slots * blk), BF16),
             pltpu.VMEM((layers, here, width), BF16),
@@ -350,10 +447,10 @@
             pltpu.VMEM(edge, BF16),
             pltpu.VMEM(edge, BF16),
             pltpu.VMEM((layers, n_sub + 1, here, width), BF16),
-            pltpu.VMEM(tall, BF16),
-            pltpu.VMEM(tall, BF16),
-            pltpu.VMEM(tall, BF16),
-            pltpu.VMEM(small, BF16),
+            pltpu.VMEM((layers, 2, n_dom // 2, wrows, units), F32),
+            pltpu.VMEM(half, F32),
+            pltpu.VMEM(half, BF16),
+            pltpu.VMEM(half, BF16),
             pltpu.VMEM(small, BF16),
             pltpu.VMEM(small, BF16),
             dma((layers, n_sub, chunks, 2)),
@@ -364,20 +461,44 @@
             dma((layers, n_dom)),
             dma((layers, n_sub, chunks)),
             dma((layers, n_sub + 1, chunks)),
-            dma((layers, n_dom)),
-            dma((layers, n_dom)),
+            dma((layers,)),
+            dma((layers,)),
+            dma((layers, n_dom // 2)),
+            dma((layers, n_dom // 2)),
             dma((layers, n_sub)),
             dma((layers, n_sub)),
             dma((layers, n_sub)),
             dma((layers, n_sub)),
-            dma((layers, n_dom)),
-            dma((layers, n_dom)),
+            dma((layers, n_dom // 2, n_sub)),
+            dma((layers, n_dom // 2, n_sub)),
+            dma((layers, n_dom // 2, n_sub)),
+            dma((layers, n_dom, n_sub)),
         ],
         compiler_params=pltpu.CompilerParams(
             collective_id=0, has_side_effects=True, vmem_limit_bytes=60 * 1024 * 1024
         ),
     )(local_blocks, remote_blocks, send_blocks, send_counts, partner, features, local_matrix,
       remote_matrix, self_weight, neighbor_weight, output_weight, output_cotangent)
+    piece = here // layers
+
+    def rows(shape):
+        return pl.BlockSpec((1,) + shape[1:], lambda i: (i,) + (0,) * (len(shape) - 1))
+
+    wide, long = (layers, width, units), (layers, units, width)
+    return pl.pallas_call(
+        functools.partial(finish, scale, wrows),
+        grid=(layers,),
+        out_shape=(
+            jax.ShapeDtypeStruct((here, width), BF16),
+            jax.ShapeDtypeStruct((here, width), F32),
+            jax.ShapeDtypeStruct(wide, F32),
+            jax.ShapeDtypeStruct(wide, F32),
+            jax.ShapeDtypeStruct(long, F32),
+        ),
+        in_specs=[pl.BlockSpec((piece, width), lambda i: (i, 0))] * 2 + [rows(full)],
+        out_specs=(pl.BlockSpec((piece, width), lambda i: (i, 0)),) * 2 + (rows(wide), rows(wide), rows(long)),
+        compiler_params=pltpu.CompilerParams(vmem_limit_bytes=32 * 1024 * 1024),
+    )(upd, fg, weights)
 
 
 def solution(mesh):

time: 119 us -> 108 us (0.908)
  Pallas kernels: 110 us -> 104 us
  local copies, waits for them, and re-layouts: 7.8 us -> 3.39 us
    pallas_call x1 -> x2, Pallas kernels: 110 us -> 104 us  [the longest x1 102 us: local(): pl.pallas_call(functools.partial(kernel, n_dom, n_sub), out_shape=(jax.Sh...]
    unnamed x11 -> x6, local copies, waits for them, and re-layouts: 7.8 us -> 3.39 us
where the time goes in v2:
time: 108 us
  Pallas kernels  104 us (96%)
  local copies, waits for them, and re-layouts  3.39 us (3%)
    pallas_call x1, Pallas kernels, local(): pl.pallas_call(functools.partial(kernel, n_dom, n_sub), out_shape=(jax.Sh...  102 us
    unnamed x6, local copies, waits for them, and re-layouts  3.39 us

profile of v2, /device:TPU:1, one launch (start us, length us, event | category | flops | bytes accessed | tf_op | source)
XLA Modules:
  0.0 107.6 jit_solution(6729037535776306693)
XLA Ops:
  0.6 101.5 %shard_map.155 = (bf16[512,256]{1,0:T(8,128)(2,1)}, f32[512,256]{1,0:T(8,128)}, bf16[2,4,4,48,512]{4,3,2,1,0:T(8,128)(2,1)}) custom-call(s32[4,4]{1,0:T(4,128)} %lb.1, s32[4,4]{1,0:T(4,128)} %rb.1, s32[1,2,2]{2,1,0:T(2,128)} %sb.1, s32[1,2]{1,0:T(1,128)} %sc.1, s32[2,4]{1,0:T(2,128)} %pt.1, bf16[512,256]{1,0:T(8,128)(2,1)} %x_ref.1, ...), custom_call_target="tpu_custom_call" | custom-call | tf_op jit(solution)/shard_map/pallas_call | solution.py:420
  102.2 0.0 copy-start
  102.2 1.4 %copy-done = bf16[2,4,4,48,512]{4,3,2,1,0:T(8,128)(2,1)S(1)} copy-done((bf16[2,4,4,48,512]{4,3,2,1,0:T(8,128)(2,1)S(1)}, bf16[2,4,4,48,512]{4,3,2,1,0:T(8,128)(2,1)}, u32[]{:S(2)}) %copy-start) | copy-done | bytes 1572888
  103.6 0.0 copy-start.1
  103.6 1.0 copy-done.1
  104.6 0.0 copy-start.2
  104.6 0.9 copy-done.2
  105.6 2.0 %shard_map.156 = (bf16[512,256]{1,0:T(8,128)(2,1)}, f32[512,256]{1,0:T(8,128)}, f32[2,256,512]{2,1,0:T(8,128)}, f32[2,256,512]{2,1,0:T(8,128)}, f32[2,512,256]{2,1,0:T(8,128)}) custom-call(bf16[512,256]{1,0:T(8,128)(2,1)S(1)} %copy-done.2, f32[512,256]{1,0:T(8,128)S(1)} %copy-done.1, bf16[2,4,4,48,512]{4,3,2,1,0:T(8,128)(2,1)S(1)} %copy-done), custom_call_target="tpu_custom_call" | custom-call | tf_op jit(solution)/shard_map/pallas_call | solution.py:488
Async XLA Ops:
  102.2 1.4 %copy-start = (bf16[2,4,4,48,512]{4,3,2,1,0:T(8,128)(2,1)S(1)}, bf16[2,4,4,48,512]{4,3,2,1,0:T(8,128)(2,1)}, u32[]{:S(2)}) copy-start(bf16[2,4,4,48,512]{4,3,2,1,0:T(8,128)(2,1)} %get-tuple-element.10.w_ref) | copy-start | bytes 4718596
  103.6 1.0 copy-start.1
  104.6 0.9 copy-start.2

commit v3 on v2

--- a/solution.py
+++ b/solution.py
@@ -30,7 +30,7 @@
     x_ref, lm_h, rm_h, ws_h, wn_h, wo_h, ct_h,
     upd, fg, wfull,
     lm, rm, ws, wn, wo, ct, in_sem,
-    adj, far, st, ag, agg, pre, hid, own,
+    adj, far, st, ag, agg, pre, hid, gh, own,
     bsend, brecv, rsend, rrecv, rs,
     wpart, crecv, xsend, xrecv, zpart, zrecv,
     ag_s, ag_r, bf_s, bf_r, bb_s, bb_r, rs_s, rs_r,
@@ -80,8 +80,8 @@
     right, left = jnp.minimum(sub + 1, n_sub - 1), jnp.maximum(sub - 1, 0)
     has_right, has_left = sub < n_sub - 1, sub > 0
 
-    def gather_start(l):
-        for c in range(chunks):
+    def gather_start(l, c):
+        for _ in (0,):
             part = st.at[l, pl.ds(c * crow, crow)]
             there = ag.at[l, sub, pl.ds(c * crow, crow)]
             start(remote(part, there, ag_s.at[l, sub, c, 0], ag_r.at[l, sub, c], "sub", right), has_right)
@@ -149,11 +149,13 @@
             @pl.when(jnp.logical_and(raw >= 0, raw < n_sub))
             def _(at=jnp.clip(raw, 0, n_sub - 1)):
                 cols = pl.ds(pl.multiple_of(at * here, here), here)
-                own[0] += dot(adj[:, cols], ag[l, at])
+                fg[...] += dot(adj[:, cols], ag[l, at])
 
     st[0] = x_ref[...]
     for l in range(layers):
-        gather_start(l)
+        if l == 0:
+            for c in range(chunks):
+                gather_start(l, c)
         boundary_start(l)
         brecv[l, dom] = jnp.zeros(brecv.shape[2:], BF16)
         if l == 0:
@@ -166,35 +168,37 @@
                 gather_step(l, 1, c)
             loads["rm"].wait()
             build(rm, far_column, far, 0, n_dom * slots)
-            loads["ws"].wait()
+            for name in ("ws", "wn", "wo", "ct"):
+                loads[name].wait()
             pre[l] = dot(st[l], ws[l])
         else:
             pre[l] = dot(st[l], ws[l])
             for c in range(chunks):
                 gather_step(l, 1, c)
-        own[0] = dot(adj[:, pl.ds(pl.multiple_of(sub * here, here), here)], st[l])
+        fg[...] = dot(adj[:, pl.ds(pl.multiple_of(sub * here, here), here)], st[l])
         for d in range(2, n_sub):
             for c in range(chunks):
                 gather_step(l, d, c)
                 if c == 0:
                     gathered(l, d - 1)
+                    if l == layers - 1 and d == 2:
+                        gh[...] = dot_nt(ct[...], wo[l])
             if d == 2:
                 arrive(brecv, bf_r, l, "dom", dom, n_dom)
-                own[0] += dot(far[...], brecv[l].reshape(-1, width))
+                fg[...] += dot(far[...], brecv[l].reshape(-1, width))
         gathered(l, n_sub - 1)
-        if l == 0:
-            loads["wn"].wait()
-            loads["wo"].wait()
-            loads["ct"].wait()
-        agg[l] = own[0].astype(BF16)
-        preact = pre[l] + dot(agg[l], wn[l])
-        pre[l] = preact
-        hid[l] = (preact / (1.0 + jnp.exp(-preact))).astype(BF16)
-        result = (st[l].astype(F32) + dot(hid[l], wo[l])).astype(BF16)
-        if l + 1 < layers:
-            st[l + 1] = result
-        else:
-            upd[...] = result
+        for c in range(chunks):
+            rows = slice(c * crow, (c + 1) * crow)
+            agg[l, rows] = fg[rows].astype(BF16)
+            preact = pre[l, rows] + dot(agg[l, rows], wn[l])
+            pre[l, rows] = preact
+            hid[l, rows] = (preact / (1.0 + jnp.exp(-preact))).astype(BF16)
+            result = (st[l, rows].astype(F32) + dot(hid[l, rows], wo[l])).astype(BF16)
+            if l + 1 < layers:
+                st[l + 1, rows] = result
+                gather_start(l + 1, c)
+            else:
+                upd[rows] = result
 
     wrows = xsend.shape[2]
     zrows = zpart.shape[2]
@@ -279,6 +283,7 @@
                 part = wfull.at[l, p, s]
                 remote(part, part, wm_s.at[l, q, s], wm_r.at[l, p, s], "dom", mate).wait_recv()
 
+    trow = width // chunks
     def reduce_start(l, ga):
         for d in range(n_sub - 1, -1, -1):
             for way in (0, 1) if d else (0,):
@@ -288,7 +293,7 @@
 
                 @pl.when(ok)
                 def _(t=t):
-                    own[t] = dot_tn(adj[:, pl.ds(pl.multiple_of(t * here, here), here)], ga)
+                    own[t] = dot(ga, adj[:, pl.ds(pl.multiple_of(t * here, here), here)])
 
                 if d:
                     edge = sub == (n_sub - 1 if way else 0)
@@ -297,7 +302,7 @@
     def reduce_send(l, t, way, cond, add):
         to = left if way else right
         for c in range(chunks):
-            rows = pl.ds(c * crow, crow)
+            rows = pl.ds(c * trow, trow)
             part = rs.at[l, t, rows]
             land = jnp.where(t == to, n_sub, t) if way else t
             copy = remote(part, rs.at[l, land, rows], rs_s.at[l, t, c], rs_r.at[l, land, c], "sub", to)
@@ -325,23 +330,24 @@
             @pl.when(cond)
             def _(slot=slot):
                 for c in range(chunks):
-                    rows = pl.ds(c * crow, crow)
+                    rows = pl.ds(c * trow, trow)
                     part = rs.at[l, slot, rows]
                     remote(part, part, rs_r.at[l, slot, c], rs_r.at[l, slot, c], "sub", left).wait_recv()
                     own[sub, rows] += rs[l, slot, rows].astype(F32)
-        return own[sub]
 
     fg[...] = ct[...].astype(F32)
     for l in range(layers - 1, -1, -1):
         cot = fg[...].astype(BF16)
         preact = pre[l]
         logistic = 1.0 / (1.0 + jnp.exp(-preact))
-        gp = (dot_nt(cot, wo[l]) * logistic * (1.0 + preact * (1.0 - logistic))).astype(BF16)
-        ga = dot_nt(gp, wn[l]).astype(BF16)
+        above = gh[...] if l == layers - 1 else dot_nt(cot, wo[l])
+        gp = (above * logistic * (1.0 + preact * (1.0 - logistic))).astype(BF16)
+        ga = dot_nt(wn[l], gp).astype(BF16)
         reduce_start(l, ga)
-        rsend[l] = dot_tn(far[...], ga).astype(BF16).reshape(rsend.shape[1:])
         for d in range(1, n_dom):
             p = lax.rem(dom + d, n_dom)
+            cols = pl.ds(pl.multiple_of(p * slots * blk, slots * blk), slots * blk)
+            rsend[l, p] = dot(ga, far[:, cols]).astype(BF16)
             start(remote(rsend.at[l, p], rrecv.at[l, dom], bb_s.at[l, p], bb_r.at[l, dom], "dom", p))
         weights_start(l, cot, gp)
         if l + 1 < layers:
@@ -356,11 +362,11 @@
             p = lax.rem(dom + d, n_dom)
             for j in range(slots):
                 ones = picks(p, j)
-                slot = rrecv[l, p, j * blk:(j + 1) * blk, :].astype(F32)
+                slot = rrecv[l, p, :, j * blk:(j + 1) * blk].astype(F32)
                 for b in range(nb):
-                    fg[b * blk:(b + 1) * blk, :] += slot * ones[b]
-        near = reduce_last(l)
-        fg[...] = fg[...] + near
+                    own[sub, :, b * blk:(b + 1) * blk] += slot * ones[b]
+        reduce_last(l)
+        fg[...] += own[sub].T
     for l in range(layers - 1, 0, -1):
         weights_back(l)
     weights_sub(0)
@@ -413,6 +419,7 @@
     vmem, smem = pl.BlockSpec(memory_space=pltpu.VMEM), pl.BlockSpec(memory_space=pltpu.SMEM)
     dma = pltpu.SemaphoreType.DMA
     edge = (layers, n_dom, slots * blk, width)
+    back = (layers, n_dom, width, slots * blk)
     half = (layers, n_dom // 2, wrows, units)
     small = (layers, n_sub, zrows, units)
     full = (layers, n_dom, n_sub, zrows, units)
@@ -441,12 +448,13 @@
             pltpu.VMEM((layers, here, width), BF16),
             pltpu.VMEM((layers, here, units), F32),
             pltpu.VMEM((layers, here, units), BF16),
-            pltpu.VMEM((n_sub, here, width), F32),
+            pltpu.VMEM((here, units), F32),
+            pltpu.VMEM((n_sub, width, here), F32),
             pltpu.VMEM(edge, BF16),
             pltpu.VMEM(edge, BF16),
-            pltpu.VMEM(edge, BF16),
-            pltpu.VMEM(edge, BF16),
-            pltpu.VMEM((layers, n_sub + 1, here, width), BF16),
+            pltpu.VMEM(back, BF16),
+            pltpu.VMEM(back, BF16),
+            pltpu.VMEM((layers, n_sub + 1, width, here), BF16),
             pltpu.VMEM((layers, 2, n_dom // 2, wrows, units), F32),
             pltpu.VMEM(half, F32),
             pltpu.VMEM(half, BF16),
@@ -497,7 +505,7 @@
         ),
         in_specs=[pl.BlockSpec((piece, width), lambda i: (i, 0))] * 2 + [rows(full)],
         out_specs=(pl.BlockSpec((piece, width), lambda i: (i, 0)),) * 2 + (rows(wide), rows(wide), rows(long)),
-        compiler_params=pltpu.CompilerParams(vmem_limit_bytes=32 * 1024 * 1024),
+        compiler_params=pltpu.CompilerParams(vmem_limit_bytes=60 * 1024 * 1024),
     )(upd, fg, weights)
 
 

time: 108 us -> 106 us (0.981)
  local copies, waits for them, and re-layouts: 3.39 us -> 0 us
    unnamed x6 -> x0, local copies, waits for them, and re-layouts: 3.39 us -> none
    pallas_call x1, Pallas kernels: 2.02 us -> 3.32 us  [local(): pl.pallas_call(functools.partial(finish, scale, wrows), grid=(layers,), o...]
where the time goes in v3:
time: 106 us; the launch traced here: 105 us
  Pallas kernels  105 us (99%)
    pallas_call x1, Pallas kernels, local(): pl.pallas_call(functools.partial(kernel, n_dom, n_sub), out_shape=(jax.Sh...  101 us
    pallas_call x1, Pallas kernels, local(): pl.pallas_call(functools.partial(finish, scale, wrows), grid=(layers,), o...  3.32 us

profile of v3, /device:TPU:1, one launch (start us, length us, event | category | flops | bytes accessed | tf_op | source)
XLA Modules:
  0.0 105.3 jit_solution(9717753074649198951)
XLA Ops:
  0.6 101.3 %shard_map.155 = (bf16[512,256]{1,0:T(8,128)(2,1)}, f32[512,256]{1,0:T(8,128)}, bf16[2,4,4,48,512]{4,3,2,1,0:T(8,128)(2,1)}) custom-call(s32[4,4]{1,0:T(4,128)} %lb.1, s32[4,4]{1,0:T(4,128)} %rb.1, s32[1,2,2]{2,1,0:T(2,128)} %sb.1, s32[1,2]{1,0:T(1,128)} %sc.1, s32[2,4]{1,0:T(2,128)} %pt.1, bf16[512,256]{1,0:T(8,128)(2,1)} %x_ref.1, ...), custom_call_target="tpu_custom_call" | custom-call | tf_op jit(solution)/shard_map/pallas_call | solution.py:427
  102.0 3.3 %shard_map.156 = (bf16[512,256]{1,0:T(8,128)(2,1)}, f32[512,256]{1,0:T(8,128)}, f32[2,256,512]{2,1,0:T(8,128)}, f32[2,256,512]{2,1,0:T(8,128)}, f32[2,512,256]{2,1,0:T(8,128)}) custom-call(bf16[512,256]{1,0:T(8,128)(2,1)} %get-tuple-element.8.u_ref, f32[512,256]{1,0:T(8,128)} %get-tuple-element.9.f_ref, bf16[2,4,4,48,512]{4,3,2,1,0:T(8,128)(2,1)} %get-tuple-element.10.w_ref), custom_call_target="tpu_custom_call" | custom-call | tf_op jit(solution)/shard_map/pallas_call | solution.py:496

commit v4 on v3

--- a/solution.py
+++ b/solution.py
@@ -317,8 +317,8 @@
 
             start(copy, cond)
 
-    def reduce_finish(l):
-        for d in range(n_sub - 1, 0, -1):
+    def reduce_finish(l, last, first):
+        for d in range(last, first - 1, -1):
             for way in (0, 1):
                 raw = sub - d if way else sub + d
                 ok = raw >= 0 if way else raw < n_sub
@@ -354,9 +354,15 @@
             weights_sub(l + 1)
         upstream = fg[...] + dot_nt(gp, ws[l])
         weights_pair(l)
-        reduce_finish(l)
+        reduce_finish(l, n_sub - 1, 2)
+        if l == 0:
+            weights_dom(l)
+        reduce_finish(l, 1, 1)
         fg[...] = upstream
-        weights_dom(l)
+        if l == 0:
+            weights_sub(l)
+            for k in range(layers - 1, 0, -1):
+                weights_back(k)
         arrive(rrecv, bb_r, l, "dom", dom, n_dom)
         for d in range(1, n_dom):
             p = lax.rem(dom + d, n_dom)
@@ -365,14 +371,14 @@
                 slot = rrecv[l, p, :, j * blk:(j + 1) * blk].astype(F32)
                 for b in range(nb):
                     own[sub, :, b * blk:(b + 1) * blk] += slot * ones[b]
+        if l == 0:
+            weights_back(l)
+            for k in range(layers - 1, 0, -1):
+                weights_pass(k)
         reduce_last(l)
+        if l > 0:
+            weights_dom(l)
         fg[...] += own[sub].T
-    for l in range(layers - 1, 0, -1):
-        weights_back(l)
-    weights_sub(0)
-    for l in range(layers - 1, 0, -1):
-        weights_pass(l)
-    weights_back(0)
     weights_pass(0)
     for l in range(layers):
         weights_done(l)

time: 106 us -> 105 us (level)
  no operation moved by 1% of the time
where the time goes in v4:
time: 105 us
  Pallas kernels  104 us (99%)
    pallas_call x1, Pallas kernels, local(): pl.pallas_call(functools.partial(kernel, n_dom, n_sub), out_shape=(jax.Sh...  101 us
    pallas_call x1, Pallas kernels, local(): pl.pallas_call(functools.partial(finish, scale, wrows), grid=(layers,), o...  3.32 us

profile of v4, /device:TPU:1, one launch (start us, length us, event | category | flops | bytes accessed | tf_op | source)
XLA Modules:
  0.0 104.9 jit_solution(16537565423355309744)
XLA Ops:
  0.6 100.9 %shard_map.155 = (bf16[512,256]{1,0:T(8,128)(2,1)}, f32[512,256]{1,0:T(8,128)}, bf16[2,4,4,48,512]{4,3,2,1,0:T(8,128)(2,1)}) custom-call(s32[4,4]{1,0:T(4,128)} %lb.1, s32[4,4]{1,0:T(4,128)} %rb.1, s32[1,2,2]{2,1,0:T(2,128)} %sb.1, s32[1,2]{1,0:T(1,128)} %sc.1, s32[2,4]{1,0:T(2,128)} %pt.1, bf16[512,256]{1,0:T(8,128)(2,1)} %x_ref.1, ...), custom_call_target="tpu_custom_call" | custom-call | tf_op jit(solution)/shard_map/pallas_call | solution.py:433
  101.6 3.3 %shard_map.156 = (bf16[512,256]{1,0:T(8,128)(2,1)}, f32[512,256]{1,0:T(8,128)}, f32[2,256,512]{2,1,0:T(8,128)}, f32[2,256,512]{2,1,0:T(8,128)}, f32[2,512,256]{2,1,0:T(8,128)}) custom-call(bf16[512,256]{1,0:T(8,128)(2,1)} %get-tuple-element.8.u_ref, f32[512,256]{1,0:T(8,128)} %get-tuple-element.9.f_ref, bf16[2,4,4,48,512]{4,3,2,1,0:T(8,128)(2,1)} %get-tuple-element.10.w_ref), custom_call_target="tpu_custom_call" | custom-call | tf_op jit(solution)/shard_map/pallas_call | solution.py:502
